TPU v7x, 32 devices: a whole 2x2x4 slice. The times are simulated.
32 devices in a mesh: groups: 2 (over y), ckpt: 4 (over z), hid: 4 (over x, core).
Axes of the slice: x: 2, y: 2, z: 4, core: 2. Of those that a mesh axis runs over, the one named last changes fastest.
Arguments:
- residual_stream: bfloat16 [4, 768, 2048], P('ckpt', ('groups', 'hid')), parts along dimension 1, may hold values from -6 to 6
- norm_gain: float32 [4, 2048], P('ckpt'), may hold values from 0.1 to 1.9
- norm_shift: float32 [4, 2048], P('ckpt'), may hold values from -3 to 3
- input_weight: bfloat16 [4, 2048, 4096], P('ckpt', None, 'hid'), may hold values from -0.125 to 0.125
- input_bias: float32 [4, 4096], P('ckpt', 'hid'), may hold values from -3 to 3
- output_weight: bfloat16 [4, 4096, 2048], P('ckpt', 'hid'), may hold values from -0.09375 to 0.09375
- output_bias: float32 [4, 2048], P('ckpt'), may hold values from -3 to 3
- encoder_weight: bfloat16 [4, 2048, 4096], P('ckpt', None, 'hid'), may hold values from -0.0625 to 0.0625
- encoder_bias: float32 [4096], P('hid'), may hold values from -3 to 3
- decoder_weight: bfloat16 [4, 4096, 2048], P('ckpt', None, 'hid'), may hold values from -0.09375 to 0.09375
- decoder_bias: float32 [4, 2048], P('ckpt', 'hid'), may hold values from -3 to 3
Outputs:
- latent_codes: bfloat16 [768, 4096], P('groups', 'hid'), parts along dimension 0
- recon_error: float32 [4, 768, 2048], P('ckpt', 'groups', 'hid'), parts along dimension 1
There are 2 independent parts, one for each index of `groups`. A program takes and returns all parts, laid end to end along the dimension named above; an argument that names none is the same for every part. Nothing has to cross between parts.
All inputs are finite; a program needn't handle non-finite values.
Results may differ from a plain program's by a relative error of at most 0.0056.
Values may be sent and summed in bfloat16 or wider, within the bound.
A program may use at most 64 MiB of HBM per device.

v0:
```python
import jax
import jax.numpy as jnp
from jax import lax
from jax.sharding import PartitionSpec as P


def per_device(
    residual_stream,
    norm_gain,
    norm_shift,
    input_weight,
    input_bias,
    output_weight,
    output_bias,
    encoder_weight,
    encoder_bias,
    decoder_weight,
    decoder_bias,
):
    values = residual_stream[0].astype(jnp.float32)
    average = jnp.mean(values, axis=-1, keepdims=True)
    centred = values - average
    variance = jnp.mean(centred * centred, axis=-1, keepdims=True)
    normed = (centred * lax.rsqrt(variance + 1e-05) * norm_gain[0] + norm_shift[0]).astype(
        jnp.bfloat16
    )
    first_weight = input_weight[0]
    first_bias = input_bias[0]
    second_weight = output_weight[0]
    hidden = jax.nn.gelu(
        jnp.dot(
            lax.all_gather(normed, "hid", axis=0, tiled=True),
            first_weight,
            preferred_element_type=jnp.float32,
        )
        + first_bias,
        approximate=False,
    ).astype(jnp.bfloat16)
    partial_out = jnp.dot(hidden, second_weight, preferred_element_type=jnp.float32)
    mlp_out = (lax.psum(partial_out, "hid") + output_bias[0]).astype(jnp.bfloat16)
    encoder_terms = jnp.dot(mlp_out, encoder_weight[0], preferred_element_type=jnp.float32)
    latent_codes = jax.nn.relu(lax.psum(encoder_terms, "ckpt") + encoder_bias).astype(jnp.bfloat16)
    local_decoder = decoder_weight[0]
    column_count = local_decoder.shape[1]
    rebuilt = (
        jnp.dot(
            lax.all_gather(latent_codes, "hid", axis=1, tiled=True),
            local_decoder,
            preferred_element_type=jnp.float32,
        )
        + decoder_bias[0]
    )
    own_columns = lax.dynamic_slice_in_dim(
        mlp_out, lax.axis_index("hid") * column_count, column_count, 1
    ).astype(jnp.float32)
    recon_error = (own_columns - rebuilt)[None]
    return (latent_codes, recon_error)


def solution(mesh):
    placed = (
        P("ckpt", ("groups", "hid"), None),
        P("ckpt", None),
        P("ckpt", None),
        P("ckpt", None, "hid"),
        P("ckpt", "hid"),
        P("ckpt", "hid", None),
        P("ckpt", None),
        P("ckpt", None, "hid"),
        P("hid"),
        P("ckpt", None, "hid"),
        P("ckpt", "hid"),
    )
    return jax.shard_map(
        per_device,
        mesh=mesh,
        in_specs=placed,
        out_specs=(P("groups", "hid"), P("ckpt", "groups", "hid")),
        check_vma=False,
    )
```

profile of v0, /device:TPU:0, one launch (start us, length us, event | category | flops | bytes accessed | tf_op | source)
XLA Modules:
  0.0 233.3 jit_solution(14858888776073998837)
XLA Ops:
  7.2 0.0 copy-start.3
  7.2 0.0 all-gather.3.cloned.1.call-start
  7.2 1.1 convert_reduce_fusion
  8.4 1.3 fusion.34
  9.7 2.1 fusion.37
  11.7 0.0 all-gather.3.cloned.1.call-update
  11.8 0.0 all-reduce.3.cloned.1.call-start
  11.8 22.5 %all-gather.3.cloned.1.call-done = bf16[384,2048]{1,0:T(8,128)(2,1)} async-done(((bf16[96,2048]{1,0:T(8,128)(2,1)}), bf16[384,2048]{1,0:T(8,128)(2,1)}) %all-gather.3.cloned.1.call-update) | async-done | bytes 1572880 | tf_op jit(solution)/shard_map/all_gather | solution.py:32
  34.3 0.0 copy-done.3
  34.3 12.3 %fusion.4 = f32[384,2048]{1,0:T(8,128)} fusion(bf16[1,1024,2048]{2,1,0:T(8,128)(2,1)} %param.16, bf16[384,2048]{1,0:T(8,128)(2,1)} %all-gather.3.cloned.1.call-done, bf16[1,2048,1024]{2,1,0:T(8,128)(2,1)} %param.14, f32[1024]{0:T(1024)S(1)} %bitcast.51), kind=kOutput, calls=%fused_computation.4 | convolution fusion | flops 3247177728 | bytes 13111296 | tf_op jit(solution)/shard_map/dot_general | solution.py:39
  46.5 0.0 copy-start
  46.5 0.0 all-reduce.3.cloned.1.call-update
  46.6 0.0 all-reduce.5.cloned.1.call-start
  46.6 68.5 %all-reduce.3.cloned.1.call-done = f32[384,2048]{1,0:T(8,128)} async-done(((f32[384,2048]{1,0:T(8,128)}), f32[384,2048]{1,0:T(8,128)}) %all-reduce.3.cloned.1.call-update) | async-done | bytes 3145744 | tf_op jit(solution)/shard_map/psum | solution.py:40
  115.1 0.0 copy-done
  115.1 0.0 copy-start.2
  115.1 2.4 %add_convert_fusion = bf16[384,2048]{1,0:T(8,128)(2,1)S(1)} fusion(f32[384,2048]{1,0:T(8,128)} %all-reduce.3.cloned.1.call-done, f32[2048]{0:T(1024)S(1)} %bitcast.50), kind=kLoop, calls=%fused_computation.8 | loop fusion | flops 1572864 | bytes 4726784 | tf_op jit(solution)/shard_map/convert_element_type | solution.py:40
  117.5 0.8 copy-done.2
  118.3 3.0 %fusion.2 = f32[384,1024]{1,0:T(8,128)} fusion(bf16[384,2048]{1,0:T(8,128)(2,1)S(1)} %add_convert_fusion, bf16[1,2048,1024]{2,1,0:T(8,128)(2,1)S(1)} %copy-done.2), kind=kOutput, calls=%fused_computation.2 | convolution fusion | flops 1610612736 | bytes 7340032 | tf_op jit(solution)/shard_map/dot_general | solution.py:41
  121.3 0.0 copy-start.1
  121.3 0.0 all-reduce.5.cloned.1.call-update
  121.3 0.0 copy-start.4
  121.3 0.0 all-gather.5.cloned.1.call-start
  121.3 69.3 %all-reduce.5.cloned.1.call-done = f32[384,1024]{1,0:T(8,128)} async-done(((f32[384,1024]{1,0:T(8,128)}), f32[384,1024]{1,0:T(8,128)}) %all-reduce.5.cloned.1.call-update) | async-done | bytes 1572880 | tf_op jit(solution)/shard_map/psum | solution.py:42
  190.7 0.0 copy-done.1
  190.7 2.5 %maximum_convert_fusion = bf16[384,1024]{1,0:T(8,128)(2,1)} fusion(f32[384,1024]{1,0:T(8,128)} %all-reduce.5.cloned.1.call-done, f32[1024]{0:T(1024)S(1)} %copy-done.1), kind=kLoop, calls=%fused_computation.13 | loop fusion | flops 1179648 | bytes 2363392 | tf_op jit(solution)/shard_map/convert_element_type | solution.py:42
  193.1 0.0 all-gather.5.cloned.1.call-update
  193.2 27.7 %all-gather.5.cloned.1.call-done = bf16[384,4096]{1,0:T(8,128)(2,1)} async-done(((bf16[384,1024]{1,0:T(8,128)(2,1)}), bf16[384,4096]{1,0:T(8,128)(2,1)}) %all-gather.5.cloned.1.call-update) | async-done | bytes 3145744 | tf_op jit(solution)/shard_map/all_gather | solution.py:47
  220.9 0.0 copy-done.4
  220.9 5.8 %fusion.26 = f32[1,384,512]{2,1,0:T(8,128)} fusion(bf16[384,4096]{1,0:T(8,128)(2,1)} %all-gather.5.cloned.1.call-done, bf16[1,4096,512]{2,1,0:T(8,128)(2,1)} %param.20, f32[512]{0:T(512)S(1)} %bitcast.52, bf16[384,2048]{1,0:T(8,128)(2,1)S(1)} %add_convert_fusion, s32[]{:T(128)S(6)} %select_n.3), kind=kOutput, calls=%fused_computation.31 | convolution fusion | flops 1611202560 | bytes 8521732 | tf_op jit(solution)/shard_map/dot_general | solution.py:46
  (2 shorter events, 0.0 us)
Async XLA Ops:
  7.2 27.1 %copy-start.3 = (f32[1,1024]{1,0:T(1,128)S(1)}, f32[1,1024]{1,0:T(1,128)}, u32[]{:S(2)}) copy-start(f32[1,1024]{1,0:T(1,128)} %param.15) | copy-start | bytes 12292
  7.2 27.1 %all-gather.3.cloned.1.call-start = ((), (), s32[]{:S(2)}) async-start(), calls=%async_computation | async-start | bytes 1966080 | tf_op jit(solution)/shard_map/all_gather | solution.py:32
  11.8 103.4 %all-reduce.3.cloned.1.call-start = ((), (), s32[]{:S(2)}) async-start(), calls=%async_computation.1 | async-start | bytes 6291456 | tf_op jit(solution)/shard_map/psum | solution.py:40
  46.5 68.6 %copy-start = (f32[1,2048]{1,0:T(1,128)S(1)}, f32[1,2048]{1,0:T(1,128)}, u32[]{:S(2)}) copy-start(f32[1,2048]{1,0:T(1,128)} %param.17) | copy-start | bytes 24580
  46.6 144.1 %all-reduce.5.cloned.1.call-start = ((), (), s32[]{:S(2)}) async-start(), calls=%async_computation.2 | async-start | bytes 3145728 | tf_op jit(solution)/shard_map/psum | solution.py:42
  115.1 3.1 %copy-start.2 = (bf16[1,2048,1024]{2,1,0:T(8,128)(2,1)S(1)}, bf16[1,2048,1024]{2,1,0:T(8,128)(2,1)}, u32[]{:S(2)}) copy-start(bf16[1,2048,1024]{2,1,0:T(8,128)(2,1)} %param.18) | copy-start | bytes 12582916
  121.3 69.4 %copy-start.1 = (f32[1024]{0:T(1024)S(1)}, f32[1024]{0:T(1024)}, u32[]{:S(2)}) copy-start(f32[1024]{0:T(1024)} %param.19) | copy-start | bytes 12292
  121.3 99.6 %copy-start.4 = (f32[1,512]{1,0:T(1,128)S(1)}, f32[1,512]{1,0:T(1,128)}, u32[]{:S(2)}) copy-start(f32[1,512]{1,0:T(1,128)} %param.21) | copy-start | bytes 6148
  121.3 99.6 %all-gather.5.cloned.1.call-start = ((), (), s32[]{:S(2)}) async-start(), calls=%async_computation.3 | async-start | bytes 3932160 | tf_op jit(solution)/shard_map/all_gather | solution.py:47
Sparse Core Ops, SparseCore 0:
  11.9 22.3 all-gather.2
  46.7 68.4 all-reduce.2
  121.4 69.2 all-reduce.4
  193.3 27.5 all-gather.4
where the time goes:
time: 233 us
  waiting for transfers between devices  188 us (81%)
  matrix products  21 us (9%)
  between operations  13.8 us (6%)
  other arithmetic  9.33 us (4%)
    psum x1, waiting for transfers between devices, per_device(): lax.psum(encoder_terms, 'ckpt') + encoder_bias  69.3 us
    psum x1, waiting for transfers between devices, per_device(): lax.psum(partial_out, 'hid') + output_bias[0]  68.5 us
    all_gather x1, waiting for transfers between devices, per_device(): lax.all_gather(latent_codes, 'hid', axis=1, tiled=True)  27.7 us
    all_gather x1, waiting for transfers between devices, per_device(): lax.all_gather(normed, 'hid', axis=0, tiled=True)  22.5 us
    dot_general x1, matrix products, per_device(): jnp.dot(hidden, second_weight, preferred_element_type=jnp.float32)  12.3 us
    dot_general x1, matrix products, per_device(): jnp.dot(lax.all_gather(latent_codes, 'hid', axis=1, tiled=True), local_de...  5.81 us
  transfers between devices with their start and end apart: 4, of which 4 were waited for; matrix products, arithmetic and copies ran while one was open for 0% of the time, Pallas kernels for 0%

commit v1 on v0

--- a/solution.py
+++ b/solution.py
@@ -37,7 +37,9 @@
         approximate=False,
     ).astype(jnp.bfloat16)
     partial_out = jnp.dot(hidden, second_weight, preferred_element_type=jnp.float32)
-    mlp_out = (lax.psum(partial_out, "hid") + output_bias[0]).astype(jnp.bfloat16)
+    mlp_out = (jnp.sum(lax.all_gather(partial_out, "hid"), axis=0) + output_bias[0]).astype(
+        jnp.bfloat16
+    )
     encoder_terms = jnp.dot(mlp_out, encoder_weight[0], preferred_element_type=jnp.float32)
     latent_codes = jax.nn.relu(lax.psum(encoder_terms, "ckpt") + encoder_bias).astype(jnp.bfloat16)
     local_decoder = decoder_weight[0]

time: 233 us -> 253 us (1.086)
  waiting for transfers between devices: 188 us -> 202 us
  other arithmetic: 9.33 us -> 13.6 us
    all_gather x0 -> x1, waiting for transfers between devices: none -> 82.2 us  [per_device(): lax.all_gather(partial_out, 'hid')]
    psum x1 -> x0, waiting for transfers between devices: 68.5 us -> none  [per_device(): lax.psum(partial_out, 'hid') + output_bias[0]]
    reduce_sum x0 -> x1, other arithmetic: none -> 6.29 us  [per_device(): jnp.sum(lax.all_gather(partial_out, 'hid'), axis=0) + output_bias[0]]
where the time goes in v1:
time: 253 us
  waiting for transfers between devices  202 us (80%)
  matrix products  21.1 us (8%)
  between operations  13.8 us (5%)
  other arithmetic  13.6 us (5%)
    all_gather x1, waiting for transfers between devices, per_device(): lax.all_gather(partial_out, 'hid')  82.2 us
    psum x1, waiting for transfers between devices, per_device(): lax.psum(encoder_terms, 'ckpt') + encoder_bias  69.2 us
    all_gather x1, waiting for transfers between devices, per_device(): lax.all_gather(latent_codes, 'hid', axis=1, tiled=True)  27.7 us
    all_gather x1, waiting for transfers between devices, per_device(): lax.all_gather(normed, 'hid', axis=0, tiled=True)  22.5 us
    dot_general x1, matrix products, per_device(): jnp.dot(hidden, second_weight, preferred_element_type=jnp.float32)  12.2 us
    reduce_sum x1, other arithmetic, per_device(): jnp.sum(lax.all_gather(partial_out, 'hid'), axis=0) + output_bias[0]  6.29 us
    dot_general x1, matrix products, per_device(): jnp.dot(lax.all_gather(latent_codes, 'hid', axis=1, tiled=True), local_de...  5.83 us
  transfers between devices with their start and end apart: 4, of which 4 were waited for; matrix products, arithmetic and copies ran while one was open for 0% of the time, Pallas kernels for 0%

profile of v1, /device:TPU:0, one launch (start us, length us, event | category | flops | bytes accessed | tf_op | source)
XLA Modules:
  0.0 252.8 jit_solution(12260555057075581981)
XLA Ops:
  7.2 0.0 copy-start.4
  7.2 0.0 all-gather.5.cloned.1.call-start
  7.2 1.1 convert_reduce_fusion
  8.4 1.3 fusion.34
  9.7 2.1 fusion.37
  11.7 0.0 all-gather.5.cloned.1.call-update
  11.8 0.0 all-gather.9.cloned.1.call-start
  11.8 22.5 %all-gather.5.cloned.1.call-done = bf16[384,2048]{1,0:T(8,128)(2,1)} async-done(((bf16[96,2048]{1,0:T(8,128)(2,1)}), bf16[384,2048]{1,0:T(8,128)(2,1)}) %all-gather.5.cloned.1.call-update) | async-done | bytes 1572880 | tf_op jit(solution)/shard_map/all_gather | solution.py:32
  34.3 0.0 copy-done.4
  34.3 12.2 %fusion.4 = f32[384,2048]{1,0:T(8,128)} fusion(bf16[1,1024,2048]{2,1,0:T(8,128)(2,1)} %param.16, bf16[384,2048]{1,0:T(8,128)(2,1)} %all-gather.5.cloned.1.call-done, bf16[1,2048,1024]{2,1,0:T(8,128)(2,1)} %param.14, f32[1024]{0:T(1024)S(1)} %bitcast.53), kind=kOutput, calls=%fused_computation.4 | convolution fusion | flops 3247177728 | bytes 13111296 | tf_op jit(solution)/shard_map/dot_general | solution.py:39
  46.5 0.0 all-gather.9.cloned.1.call-update
  46.5 0.0 all-reduce.2.cloned.1.call-start
  46.6 82.2 %all-gather.9.cloned.1.call-done = f32[1536,2048]{1,0:T(8,128)} async-done(((f32[384,2048]{1,0:T(8,128)}), f32[1536,2048]{1,0:T(8,128)}) %all-gather.9.cloned.1.call-update) | async-done | bytes 12582928 | tf_op jit(solution)/shard_map/all_gather | solution.py:40
  128.8 0.0 copy-start.1
  128.8 6.3 %reduce_sum.29 = f32[384,2048]{1,0:T(8,128)S(1)} reduce(f32[4,384,2048]{2,1,0:T(8,128)} %bitcast.49, f32[]{:T(128)} %constant.36.clone.1), dimensions={0}, to_apply=%region_2.0 | reduce | flops 2359296 | bytes 15728644 | tf_op jit(solution)/shard_map/reduce_sum | solution.py:40
  135.1 0.0 copy-done.1
  135.1 0.0 copy-start.3
  135.1 0.3 add_convert_fusion
  135.5 0.0 copy-start
  135.5 1.1 copy-done
  136.6 1.3 copy-done.3
  137.9 3.0 %fusion.2 = f32[384,1024]{1,0:T(8,128)} fusion(bf16[384,2048]{1,0:T(8,128)(2,1)S(1)} %add_convert_fusion, bf16[1,2048,1024]{2,1,0:T(8,128)(2,1)S(1)} %copy-done.3), kind=kOutput, calls=%fused_computation.2 | convolution fusion | flops 1610612736 | bytes 7340032 | tf_op jit(solution)/shard_map/dot_general | solution.py:43
  140.9 0.0 all-reduce.2.cloned.1.call-update
  140.9 0.0 copy-start.5
  140.9 0.0 all-gather.7.cloned.1.call-start
  140.9 69.2 %all-reduce.2.cloned.1.call-done = f32[384,1024]{1,0:T(8,128)} async-done(((f32[384,1024]{1,0:T(8,128)}), f32[384,1024]{1,0:T(8,128)}) %all-reduce.2.cloned.1.call-update) | async-done | bytes 1572880 | tf_op jit(solution)/shard_map/psum | solution.py:44
  210.2 0.0 copy-done.2
  210.2 2.5 maximum_convert_fusion
  212.6 0.0 all-gather.7.cloned.1.call-update
  212.7 27.7 %all-gather.7.cloned.1.call-done = bf16[384,4096]{1,0:T(8,128)(2,1)} async-done(((bf16[384,1024]{1,0:T(8,128)(2,1)}), bf16[384,4096]{1,0:T(8,128)(2,1)}) %all-gather.7.cloned.1.call-update) | async-done | bytes 3145744 | tf_op jit(solution)/shard_map/all_gather | solution.py:49
  240.4 0.0 copy-done.5
  240.4 5.8 %fusion.26 = f32[1,384,512]{2,1,0:T(8,128)} fusion(bf16[384,4096]{1,0:T(8,128)(2,1)} %all-gather.7.cloned.1.call-done, bf16[1,4096,512]{2,1,0:T(8,128)(2,1)} %param.20, f32[512]{0:T(512)S(1)} %bitcast.54, bf16[384,2048]{1,0:T(8,128)(2,1)} %copy-done, s32[]{:T(128)S(6)} %select_n.3), kind=kOutput, calls=%fused_computation.31 | convolution fusion | flops 1611202560 | bytes 8521732 | tf_op jit(solution)/shard_map/dot_general | solution.py:48
  (3 shorter events, 0.0 us)
Async XLA Ops:
  7.2 27.1 %copy-start.4 = (f32[1,1024]{1,0:T(1,128)S(1)}, f32[1,1024]{1,0:T(1,128)}, u32[]{:S(2)}) copy-start(f32[1,1024]{1,0:T(1,128)} %param.15) | copy-start | bytes 12292
  7.2 27.1 %all-gather.5.cloned.1.call-start = ((), (), s32[]{:S(2)}) async-start(), calls=%async_computation | async-start | bytes 1966080 | tf_op jit(solution)/shard_map/all_gather | solution.py:32
  11.8 117.1 %all-gather.9.cloned.1.call-start = ((), (), s32[]{:S(2)}) async-start(), calls=%async_computation.3 | async-start | bytes 15728640 | tf_op jit(solution)/shard_map/all_gather | solution.py:40
  46.5 163.6 %all-reduce.2.cloned.1.call-start = ((), (), s32[]{:S(2)}) async-start(), calls=%async_computation.1 | async-start | bytes 3145728 | tf_op jit(solution)/shard_map/psum | solution.py:44
  128.8 6.3 %copy-start.1 = (f32[1,2048]{1,0:T(1,128)S(1)}, f32[1,2048]{1,0:T(1,128)}, u32[]{:S(2)}) copy-start(f32[1,2048]{1,0:T(1,128)} %param.17) | copy-start | bytes 24580
  135.1 2.8 %copy-start.3 = (bf16[1,2048,1024]{2,1,0:T(8,128)(2,1)S(1)}, bf16[1,2048,1024]{2,1,0:T(8,128)(2,1)}, u32[]{:S(2)}) copy-start(bf16[1,2048,1024]{2,1,0:T(8,128)(2,1)} %param.18) | copy-start | bytes 12582916
  135.5 1.2 copy-start
  140.9 69.3 %copy-start.2 = (f32[1024]{0:T(1024)S(1)}, f32[1024]{0:T(1024)}, u32[]{:S(2)}) copy-start(f32[1024]{0:T(1024)} %param.19) | copy-start | bytes 12292
  140.9 99.5 %copy-start.5 = (f32[1,512]{1,0:T(1,128)S(1)}, f32[1,512]{1,0:T(1,128)}, u32[]{:S(2)}) copy-start(f32[1,512]{1,0:T(1,128)} %param.21) | copy-start | bytes 6148
  140.9 99.5 %all-gather.7.cloned.1.call-start = ((), (), s32[]{:S(2)}) async-start(), calls=%async_computation.2 | async-start | bytes 3932160 | tf_op jit(solution)/shard_map/all_gather | solution.py:49
Sparse Core Ops, SparseCore 0:
  11.9 22.3 all-gather.4
  46.7 82.1 all-gather.8
  141.0 69.0 all-reduce.1
  212.8 27.5 all-gather.6

commit v2 on v0

--- a/solution.py
+++ b/solution.py
@@ -2,6 +2,18 @@
 import jax.numpy as jnp
 from jax import lax
 from jax.sharding import PartitionSpec as P
+
+
+def gather_by_bits(x, axis, dim):
+    ways, here = (lax.axis_size(axis), lax.axis_index(axis))
+    grown, reach = (x, 1)
+    while reach < ways:
+        theirs = lax.ppermute(grown, axis, [(d, d ^ reach) for d in range(ways)])
+        mine_first = jnp.concatenate([grown, theirs], axis=dim)
+        theirs_first = jnp.concatenate([theirs, grown], axis=dim)
+        grown = jnp.where(here & reach == 0, mine_first, theirs_first)
+        reach = 2 * reach
+    return grown
 
 
 def per_device(
@@ -44,7 +56,7 @@
     column_count = local_decoder.shape[1]
     rebuilt = (
         jnp.dot(
-            lax.all_gather(latent_codes, "hid", axis=1, tiled=True),
+            gather_by_bits(latent_codes, "hid", 1),
             local_decoder,
             preferred_element_type=jnp.float32,
         )

time: 233 us -> 247 us (1.060)
  waiting for transfers between devices: 188 us -> 198 us
    ppermute x0 -> x2, waiting for transfers between devices: none -> 37.5 us  [gather_by_bits(): theirs = lax.ppermute(grown, axis, [(d, d ^ reach) for d in range(ways)])]
    all_gather x1 -> x0, waiting for transfers between devices: 27.7 us -> none  [per_device(): lax.all_gather(latent_codes, 'hid', axis=1, tiled=True)]
  transfers between devices with their start and end apart: 4 -> 5, of which waited for: 4 -> 5; matrix products, arithmetic and copies ran while one was open for 0% -> 0% of each run, Pallas kernels for 0% -> 0%
where the time goes in v2:
time: 247 us
  waiting for transfers between devices  198 us (80%)
  matrix products  22.2 us (9%)
  between operations  13.8 us (6%)
  other arithmetic  10.2 us (4%)
    psum x1, waiting for transfers between devices, per_device(): lax.psum(encoder_terms, 'ckpt') + encoder_bias  69.4 us
    psum x1, waiting for transfers between devices, per_device(): lax.psum(partial_out, 'hid') + output_bias[0]  68.6 us
    ppermute x2, waiting for transfers between devices, gather_by_bits(): theirs = lax.ppermute(grown, axis, [(d, d ^ reach) for d in range(ways)])  37.5 us
    all_gather x1, waiting for transfers between devices, per_device(): lax.all_gather(normed, 'hid', axis=0, tiled=True)  22.5 us
    dot_general x1, matrix products, per_device(): jnp.dot(hidden, second_weight, preferred_element_type=jnp.float32)  12.3 us
    dot_general x1, matrix products, per_device(): jnp.dot(gather_by_bits(latent_codes, 'hid', 1), local_decoder, preferred_...  6.95 us
  transfers between devices with their start and end apart: 5, of which 5 were waited for; matrix products, arithmetic and copies ran while one was open for 0% of the time, Pallas kernels for 0%

profile of v2, /device:TPU:0, one launch (start us, length us, event | category | flops | bytes accessed | tf_op | source)
XLA Modules:
  0.0 246.6 jit_solution(1896454708840933690)
XLA Ops:
  7.2 0.0 copy-start.4
  7.2 0.0 all-gather.2.cloned.1.call-start
  7.2 1.1 convert_reduce_fusion
  8.4 1.3 fusion.40
  9.7 2.1 fusion.43
  11.7 0.0 all-gather.2.cloned.1.call-update
  11.8 0.0 all-reduce.3.cloned.1.call-start
  11.8 22.5 %all-gather.2.cloned.1.call-done = bf16[384,2048]{1,0:T(8,128)(2,1)} async-done(((bf16[96,2048]{1,0:T(8,128)(2,1)}), bf16[384,2048]{1,0:T(8,128)(2,1)}) %all-gather.2.cloned.1.call-update) | async-done | bytes 1572880 | tf_op jit(solution)/shard_map/all_gather | solution.py:44
  34.3 0.0 copy-done.4
  34.3 12.3 %fusion.4 = f32[384,2048]{1,0:T(8,128)} fusion(bf16[1,1024,2048]{2,1,0:T(8,128)(2,1)} %param.16, bf16[384,2048]{1,0:T(8,128)(2,1)} %all-gather.2.cloned.1.call-done, bf16[1,2048,1024]{2,1,0:T(8,128)(2,1)} %param.14, f32[1024]{0:T(1024)S(1)} %bitcast.50), kind=kOutput, calls=%fused_computation.4 | convolution fusion | flops 3247177728 | bytes 13111296 | tf_op jit(solution)/shard_map/dot_general | solution.py:51
  46.5 0.0 copy-start.1
  46.5 0.0 all-reduce.3.cloned.1.call-update
  46.6 0.0 all-reduce.5.cloned.1.call-start
  46.6 68.6 %all-reduce.3.cloned.1.call-done = f32[384,2048]{1,0:T(8,128)} async-done(((f32[384,2048]{1,0:T(8,128)}), f32[384,2048]{1,0:T(8,128)}) %all-reduce.3.cloned.1.call-update) | async-done | bytes 3145744 | tf_op jit(solution)/shard_map/psum | solution.py:52
  115.2 0.0 copy-done.1
  115.2 2.4 add_convert_fusion
  117.5 0.8 copy-done.3
  118.3 3.0 %fusion.2 = f32[384,1024]{1,0:T(8,128)} fusion(bf16[384,2048]{1,0:T(8,128)(2,1)S(1)} %add_convert_fusion, bf16[1,2048,1024]{2,1,0:T(8,128)(2,1)S(1)} %copy-done.3), kind=kOutput, calls=%fused_computation.2 | convolution fusion | flops 1610612736 | bytes 7340032 | tf_op jit(solution)/shard_map/dot_general | solution.py:53
  121.3 0.0 all-reduce.5.cloned.1.call-update
  121.3 69.4 %all-reduce.5.cloned.1.call-done = f32[384,1024]{1,0:T(8,128)} async-done(((f32[384,1024]{1,0:T(8,128)}), f32[384,1024]{1,0:T(8,128)}) %all-reduce.5.cloned.1.call-update) | async-done | bytes 1572880 | tf_op jit(solution)/shard_map/psum | solution.py:54
  190.7 0.0 copy-done.2
  190.7 1.6 maximum_convert_fusion
  192.3 0.0 copy-start
  192.3 0.1 collective-permute-start
  192.4 0.0 copy-start.5
  192.4 2.3 collective-permute-done
  194.6 1.8 maximum_select_fusion.2
  196.4 0.0 copy-done
  196.4 1.5 collective-permute-start.1
  197.9 35.3 %collective-permute-done.1 = bf16[384,2048]{1,0:T(8,128)(2,1)} collective-permute-done((bf16[384,2048]{1,0:T(8,128)(2,1)}, bf16[384,2048]{1,0:T(8,128)(2,1)}, u32[]{:S(2)}, u32[]{:S(2)}) %collective-permute-start.1) | collective-permute-done | bytes 1572896 | tf_op jit(solution)/shard_map/ppermute | solution.py:11
  233.1 0.0 copy-done.5
  233.1 6.9 %fusion.32 = f32[1,384,512]{2,1,0:T(8,128)} fusion(bf16[1,4096,512]{2,1,0:T(8,128)(2,1)} %param.20, bf16[384,2048]{1,0:T(8,128)(2,1)} %collective-permute-done.1, bf16[384,2048]{1,0:T(8,128)(2,1)} %maximum_select_fusion.2, pred[]{:T(512)S(6)} %eq.6, f32[512]{0:T(512)S(1)} %bitcast.51, bf16[384,2048]{1,0:T(8,128)(2,1)S(1)} %add_convert_fusion, s32[]{:T(128)S(6)} %select_n.19), kind=kOutput, calls=%fused_computation.39 | convolution fusion | flops 1625358336 | bytes 8521733 | tf_op jit(solution)/shard_map/dot_general | solution.py:58
  (4 shorter events, 0.0 us)
Async XLA Ops:
  7.2 27.1 %copy-start.4 = (f32[1,1024]{1,0:T(1,128)S(1)}, f32[1,1024]{1,0:T(1,128)}, u32[]{:S(2)}) copy-start(f32[1,1024]{1,0:T(1,128)} %param.15) | copy-start | bytes 12292
  7.2 27.1 %all-gather.2.cloned.1.call-start = ((), (), s32[]{:S(2)}) async-start(), calls=%async_computation | async-start | bytes 1966080 | tf_op jit(solution)/shard_map/all_gather | solution.py:44
  11.8 103.4 %all-reduce.3.cloned.1.call-start = ((), (), s32[]{:S(2)}) async-start(), calls=%async_computation.1 | async-start | bytes 6291456 | tf_op jit(solution)/shard_map/psum | solution.py:52
  46.5 68.6 %copy-start.1 = (f32[1,2048]{1,0:T(1,128)S(1)}, f32[1,2048]{1,0:T(1,128)}, u32[]{:S(2)}) copy-start(f32[1,2048]{1,0:T(1,128)} %param.17) | copy-start | bytes 24580
  46.6 144.1 %all-reduce.5.cloned.1.call-start = ((), (), s32[]{:S(2)}) async-start(), calls=%async_computation.2 | async-start | bytes 3145728 | tf_op jit(solution)/shard_map/psum | solution.py:54
  115.2 3.1 %copy-start.3 = (bf16[1,2048,1024]{2,1,0:T(8,128)(2,1)S(1)}, bf16[1,2048,1024]{2,1,0:T(8,128)(2,1)}, u32[]{:S(2)}) copy-start(bf16[1,2048,1024]{2,1,0:T(8,128)(2,1)} %param.18) | copy-start | bytes 12582916
  121.3 69.4 %copy-start.2 = (f32[1024]{0:T(1024)S(1)}, f32[1024]{0:T(1024)}, u32[]{:S(2)}) copy-start(f32[1024]{0:T(1024)} %param.19) | copy-start | bytes 12292
  192.3 4.1 %copy-start = (bf16[384,1024]{1,0:T(8,128)(2,1)}, bf16[384,1024]{1,0:T(8,128)(2,1)S(1)}, u32[]{:S(2)}) copy-start(bf16[384,1024]{1,0:T(8,128)(2,1)S(1)} %maximum_convert_fusion) | copy-start | bytes 2359300
  192.3 2.4 collective-permute-start
  192.4 40.8 %copy-start.5 = (f32[1,512]{1,0:T(1,128)S(1)}, f32[1,512]{1,0:T(1,128)}, u32[]{:S(2)}) copy-start(f32[1,512]{1,0:T(1,128)} %param.21) | copy-start | bytes 6148
  196.4 36.8 %collective-permute-start.1 = (bf16[384,2048]{1,0:T(8,128)(2,1)}, bf16[384,2048]{1,0:T(8,128)(2,1)}, u32[]{:S(2)}, u32[]{:S(2)}) collective-permute-start(bf16[384,2048]{1,0:T(8,128)(2,1)} %maximum_select_fusion.2), channel_id=1, source_target_pairs={{0,2},{1,3},{2,0},{3,1},{4,6},{5,7},{6,4},{7,5},{8,10},{9,11},{10,... | collective-permute-start | bytes 4718600 | tf_op jit(solution)/shard_map/ppermute | solution.py:11
Sparse Core Ops, SparseCore 0:
  11.9 22.3 all-gather.1
  46.7 68.4 all-reduce.2
  121.4 69.2 all-reduce.4
